TPU v7x, 512 devices: a whole 4x4x16 slice. The times are simulated.
512 devices in a mesh: gx: 32 (over z, core), gy: 16 (over x, y).
Axes of the slice: x: 4, y: 4, z: 16, core: 2. Of those that a mesh axis runs over, the one named last changes fastest.
Arguments:
- adjoint: float32 [3, 8, 512, 2048], P(None, None, 'gx', 'gy'), may hold values from -12 to 12
- checkpoints: bfloat16 [1, 3, 8, 512, 2048], P(None, None, None, 'gx', 'gy'), may hold values from -3 to 3
- wall_faces: int32 [2, 64, 256], P(None, 'gx', 'gy'), may hold values 0 or 1
Outputs:
- velocity: float32 [3, 8, 512, 2048], P(None, None, 'gx', 'gy')
- pressure: float32 [8, 512, 2048], P(None, 'gx', 'gy')
Inputs may be any that keep to these rules, and one draw needn't show every extreme that they name: `wall_faces`: 1 marks a no-slip face, 0 an open one.
All inputs are finite; a program needn't handle non-finite values. No bound on the sum of `wall_faces` on one device may be relied on, other than what follows from the above.
Results may differ from a plain program's by a relative error of at most 0.0003.
Values sent between devices are 32-bit elements; how exact they have to be, the bound alone decides.
No kernel may reach another device: no remote copies, remote signals or barrier semaphores. Data moves between devices by JAX's collectives and lax.ppermute only.
A program may use at most 64 MiB of HBM per device.

v0:
```python
import jax
import jax.numpy as jnp
import numpy as np
from jax import lax
from jax.sharding import PartitionSpec as P

ITERS = 4
node_points = np.array(
    [
        -1.0,
        -0.8717401485096066,
        -0.5917001814331423,
        -0.2092992179024789,
        0.2092992179024789,
        0.5917001814331423,
        0.8717401485096066,
        1.0,
    ]
)
node_weights = np.array(
    [
        0.03571428571428571,
        0.2107042271435061,
        0.3411226924835044,
        0.4124587946587038,
        0.4124587946587038,
        0.3411226924835044,
        0.2107042271435061,
        0.03571428571428571,
    ]
)
time_step = 0.05
viscosity = 0.02
highest = lax.Precision.HIGHEST


def with_halo(value, sides, width):
    for axis, dim in sides:
        size, length = (lax.axis_size(axis), value.shape[dim])
        up = [(i, (i + 1) % size) for i in range(size)]
        down = [(j, i) for i, j in up]
        last = lax.slice_in_dim(value, length - width, length, axis=dim)
        initial = lax.slice_in_dim(value, 0, width, axis=dim)
        before = lax.ppermute(last, axis, up)
        after = lax.ppermute(initial, axis, down)
        value = jnp.concatenate([before, value, after], axis=dim)
    return value


def derivative_table(points):
    identity = np.eye(points.shape[0])
    spacing = points[:, None] - points[None, :] + identity
    barycentric = 1.0 / np.prod(spacing, axis=1)
    matrix = barycentric[None, :] / barycentric[:, None] / spacing
    matrix = matrix * (1.0 - identity)
    return matrix - identity * np.sum(matrix, axis=1)[:, None]


def along_rows(nodal, matrix):
    blocked = jnp.asarray(np.kron(np.eye(nodal.shape[2] // 8), matrix), jnp.float32)
    return jnp.einsum("xk,czky->czxy", blocked, nodal, precision=highest)


def along_columns(nodal, matrix):
    size_y = nodal.shape[3]
    block_width = 128 if size_y % 128 == 0 else size_y
    blocked = jnp.asarray(np.kron(np.eye(block_width // 8), matrix).T, jnp.float32)
    grouped = nodal.reshape(
        nodal.shape[0], nodal.shape[1], nodal.shape[2], size_y // block_width, block_width
    )
    result = jnp.einsum("czxgk,kb->czxgb", grouped, blocked, precision=highest)
    return result.reshape(nodal.shape)


def along_depth(nodal, matrix):
    return jnp.einsum("ck,akxy->acxy", jnp.asarray(matrix, jnp.float32), nodal, precision=highest)


def mass_weights(size_x, size_y):
    weights = jnp.asarray(node_weights, jnp.float32)
    across_x = jnp.tile(weights, size_x // 8)
    across_y = jnp.tile(weights, size_y // 8)
    return weights[:, None, None] * across_x[None, :, None] * across_y[None, None, :]


def edge_flags(length):
    place = jnp.arange(length) % 8
    return ((place == 0) | (place == 7)).astype(jnp.float32)


def share_counts(size_x, size_y):
    return (1.0 + edge_flags(size_x))[:, None] * (1.0 + edge_flags(size_y))[None, :]


def boundary_masks(wall_faces, size_x, size_y):
    walls = jnp.repeat(jnp.repeat(wall_faces.astype(jnp.float32), 8, axis=1), 8, axis=2)
    interior = (1.0 - edge_flags(size_x))[:, None] * (1.0 - edge_flags(size_y))[None, :]
    middle = jnp.ones((6, size_x, size_y), jnp.float32)
    velocity_mask = jnp.concatenate(
        [(interior * (1.0 - walls[0]))[None], middle, (interior * (1.0 - walls[1]))[None]], axis=0
    )
    pressure_mask = jnp.concatenate(
        [(interior * walls[0])[None], middle, (interior * walls[1])[None]], axis=0
    )
    return (velocity_mask, pressure_mask)


def sum_rows(padded):
    size_x = padded.shape[2] - 2
    place = jnp.arange(size_x) % 8
    upper = (place == 7).astype(jnp.float32)[:, None]
    lower = (place == 0).astype(jnp.float32)[:, None]
    return padded[:, :, 1:-1, :] + upper * padded[:, :, 2:, :] + lower * padded[:, :, :-2, :]


def sum_columns(padded):
    size_y = padded.shape[3] - 2
    place = jnp.arange(size_y) % 8
    upper = (place == 7).astype(jnp.float32)
    lower = (place == 0).astype(jnp.float32)
    return padded[:, :, :, 1:-1] + upper * padded[:, :, :, 2:] + lower * padded[:, :, :, :-2]


def assemble_velocity(nodal):
    padded = with_halo(nodal, (("gx", 2), ("gy", 3)), 1)
    return sum_columns(sum_rows(padded))


def assemble_pressure(nodal):
    padded = with_halo(nodal, (("gx", 2), ("gy", 3)), 1)
    return sum_columns(sum_rows(padded))


def stiffness(nodal, wmass):
    derivative = derivative_table(node_points)
    transposed = derivative.T
    return (
        along_rows(wmass * along_rows(nodal, derivative), transposed)
        + along_columns(wmass * along_columns(nodal, derivative), transposed)
        + along_depth(wmass * along_depth(nodal, derivative), transposed)
    )


def inner(former, latter, inverse_share):
    return jnp.sum(former * latter * inverse_share)


def solve_pressure(source, pressure_mask, wmass, inverse_share):
    pressure = jnp.zeros_like(source)
    resid = source
    direction = source
    norm_now = jnp.zeros((), jnp.float32)
    for round_index in range(ITERS):
        image = pressure_mask * assemble_pressure(stiffness(direction, wmass))
        if round_index == 0:
            norm_now, curve = lax.psum(
                (inner(resid, resid, inverse_share), inner(direction, image, inverse_share)),
                ("gx", "gy"),
            )
        else:
            curve = lax.psum(inner(direction, image, inverse_share), ("gx", "gy"))
        step_length = norm_now / curve
        pressure = pressure + step_length * direction
        resid = resid - step_length * image
        if round_index + 1 < ITERS:
            norm_next = lax.psum(inner(resid, resid, inverse_share), ("gx", "gy"))
            direction = resid + norm_next / norm_now * direction
            norm_now = norm_next
    return pressure


def adjoint_step(velocity, forward, velocity_mask, pressure_mask, wmass, amass, inverse_share):
    derivative = derivative_table(node_points)
    flow = forward.astype(jnp.float32)
    flow_dx = along_rows(flow, derivative)
    flow_dy = along_columns(flow, derivative)
    flow_dz = along_depth(flow, derivative)
    velocity_dx = along_rows(velocity, derivative)
    velocity_dy = along_columns(velocity, derivative)
    velocity_dz = along_depth(velocity, derivative)
    transport = flow[0:1] * velocity_dx + flow[1:2] * velocity_dy + flow[2:3] * velocity_dz
    stretch = jnp.concatenate(
        [
            jnp.sum(velocity * flow_dx, axis=0, keepdims=True),
            jnp.sum(velocity * flow_dy, axis=0, keepdims=True),
            jnp.sum(velocity * flow_dz, axis=0, keepdims=True),
        ],
        axis=0,
    )
    advect = transport - stretch
    forcing = wmass * (velocity + time_step * advect) - time_step * viscosity * stiffness(
        velocity, wmass
    )
    moved = velocity_mask * assemble_velocity(forcing) / amass
    diverge = (
        along_rows(moved[0:1], derivative)
        + along_columns(moved[1:2], derivative)
        + along_depth(moved[2:3], derivative)
    )
    source = -pressure_mask * assemble_pressure(wmass * diverge)
    pressure = solve_pressure(source, pressure_mask, wmass, inverse_share)
    slopes = jnp.concatenate(
        [
            along_rows(pressure, derivative),
            along_columns(pressure, derivative),
            along_depth(pressure, derivative),
        ],
        axis=0,
    )
    correction = assemble_velocity(wmass * slopes) / amass
    return (velocity_mask * (moved - correction), pressure)


def local(adjoint, checkpoints, wall_faces):
    size_x = adjoint.shape[2]
    size_y = adjoint.shape[3]
    wmass = mass_weights(size_x, size_y)
    counts = share_counts(size_x, size_y)
    inverse_share = 1.0 / counts
    amass = wmass * counts
    velocity_mask, pressure_mask = boundary_masks(wall_faces, size_x, size_y)
    velocity = adjoint
    velocity, pressure = adjoint_step(
        velocity, checkpoints[0], velocity_mask, pressure_mask, wmass, amass, inverse_share
    )
    return (velocity, pressure[0])


def solution(mesh):
    return jax.shard_map(
        local,
        mesh=mesh,
        in_specs=(P(None, None, "gx", "gy"), P(None, None, None, "gx", "gy"), P(None, "gx", "gy")),
        out_specs=(P(None, None, "gx", "gy"), P(None, "gx", "gy")),
        check_vma=False,
    )
```

profile of v0, /device:TPU:1, one launch (start us, length us, event | category | flops | bytes accessed | tf_op | source)
XLA Modules:
  0.0 876.8 jit_solution(5244411411854615604)
XLA Ops:
  0.7 0.7 copy-done.11
  1.3 1.3 convolution_bitcast_fusion.3
  4.1 0.6 copy-done.15
  6.4 0.7 copy-done.13
  9.0 3.0 collective-permute-start
  12.1 3.9 collective-permute-start.1
  17.0 1.9 collective-permute-start.2
  18.9 6.7 collective-permute-start.3
  25.6 2.2 collective-permute-done.2
  27.8 1.5 collective-permute-done.3
  30.0 0.8 copy-done.1
  32.4 1.8 collective-permute-start.4
  34.3 3.5 collective-permute-start.5
  37.8 0.6 collective-permute-done.4
  38.7 1.9 collective-permute-start.6
  40.6 7.4 collective-permute-start.7
  48.1 1.6 collective-permute-done.7
  50.9 0.7 copy-done.3
  53.3 6.4 collective-permute-start.9
  59.7 0.6 collective-permute-done.8
  60.6 1.9 collective-permute-start.10
  62.6 7.4 collective-permute-start.11
  70.0 1.6 collective-permute-done.11
  71.8 0.8 multiply_reduce_fusion.5
  72.6 108.5 %all-reduce = (f32[]{:T(128)}, f32[]{:T(128)}) all-reduce(f32[]{:T(128)} %get-tuple-element.3, f32[]{:T(128)} %get-tuple-element.2), channel_id=1, replica_groups=mesh['gx'=32,'gy'=16] {'gx','gy'}, use_global_device_ids=true, to_apply=%region_4.5 | all-reduce | flops 2 | bytes 16 | tf_op jit(solution)/shard_map/psum | solution.py:156
  182.5 0.7 multiply_reduce_fusion.4
  183.2 98.5 %psum.58 = f32[]{:T(128)} all-reduce(f32[]{:T(128)} %multiply_reduce_fusion.4), channel_id=1, replica_groups=mesh['gx'=32,'gy'=16] {'gx','gy'}, use_global_device_ids=true, to_apply=%region_8.9 | all-reduce | flops 1 | bytes 8 | tf_op jit(solution)/shard_map/psum | solution.py:166
  284.5 2.3 collective-permute-start.12
  286.8 0.8 collective-permute-done.12
  287.6 2.3 collective-permute-done.13
  289.9 2.2 collective-permute-start.14
  292.2 6.4 collective-permute-start.15
  298.6 1.4 collective-permute-done.14
  299.9 0.9 collective-permute-done.15
  301.1 0.7 multiply_reduce_fusion.3
  301.8 102.7 %psum.59 = f32[]{:T(128)} all-reduce(f32[]{:T(128)} %get-tuple-element.10), channel_id=1, replica_groups=mesh['gx'=32,'gy'=16] {'gx','gy'}, use_global_device_ids=true, to_apply=%region_10.11 | all-reduce | flops 1 | bytes 8 | tf_op jit(solution)/shard_map/psum | solution.py:161
  405.9 0.7 multiply_reduce_fusion.2
  406.6 99.3 %psum.60 = f32[]{:T(128)} all-reduce(f32[]{:T(128)} %get-tuple-element.8), channel_id=1, replica_groups=mesh['gx'=32,'gy'=16] {'gx','gy'}, use_global_device_ids=true, to_apply=%region_12.13 | all-reduce | flops 1 | bytes 8 | tf_op jit(solution)/shard_map/psum | solution.py:166
  508.6 1.4 collective-permute-start.16
  510.1 0.8 collective-permute-done.16
  510.8 2.3 collective-permute-done.17
  513.3 2.3 collective-permute-start.18
  515.6 6.3 collective-permute-start.19
  522.4 1.1 collective-permute-done.19
  523.8 0.7 multiply_reduce_fusion.1
  524.5 104.3 %psum.61 = f32[]{:T(128)} all-reduce(f32[]{:T(128)} %get-tuple-element.6), channel_id=1, replica_groups=mesh['gx'=32,'gy'=16] {'gx','gy'}, use_global_device_ids=true, to_apply=%region_14.15 | all-reduce | flops 1 | bytes 8 | tf_op jit(solution)/shard_map/psum | solution.py:161
  630.8 98.4 %psum.62 = f32[]{:T(128)} all-reduce(f32[]{:T(128)} %multiply_reduce_fusion), channel_id=1, replica_groups=mesh['gx'=32,'gy'=16] {'gx','gy'}, use_global_device_ids=true, to_apply=%region_16.17 | all-reduce | flops 1 | bytes 8 | tf_op jit(solution)/shard_map/psum | solution.py:166
  731.9 2.3 collective-permute-start.20
  734.3 0.8 collective-permute-done.20
  735.0 2.3 collective-permute-done.21
  737.4 2.5 collective-permute-start.22
  739.9 6.1 collective-permute-start.23
  746.0 1.4 collective-permute-done.22
  747.4 0.9 collective-permute-done.23
  748.6 0.7 fusion.73
  749.3 102.6 %psum.63 = f32[]{:T(128)} all-reduce(f32[]{:T(128)} %fusion.73), channel_id=1, replica_groups=mesh['gx'=32,'gy'=16] {'gx','gy'}, use_global_device_ids=true, to_apply=%region_18.19 | all-reduce | flops 1 | bytes 8 | tf_op jit(solution)/shard_map/psum | solution.py:161
  854.3 2.7 collective-permute-start.24
  857.0 0.8 collective-permute-done.24
  857.8 2.3 collective-permute-done.25
  860.3 1.9 collective-permute-start.26
  862.2 6.7 collective-permute-start.27
  868.9 5.4 collective-permute-done.26
  874.3 1.0 collective-permute-done.27
  875.8 1.0 fusion.35
  (159 shorter events, 20.0 us)
Async XLA Ops:
  0.6 0.7 copy-start.11
  1.3 1.3 copy-start
  1.3 1.3 copy-start.2
  2.7 0.8 copy-start.6
  4.1 0.7 copy-start.15
  4.9 0.7 copy-start.12
  6.4 0.7 copy-start.13
  7.1 0.7 copy-start.14
  7.7 0.8 copy-start.10
  9.0 7.6 collective-permute-start
  12.1 3.9 copy-start.16
  12.1 4.7 collective-permute-start.1
  17.0 10.8 %collective-permute-start.2 = (f32[3,8,18,1]{3,2,1,0:T(8,128)S(1)}, f32[3,8,18,1]{3,2,1,0:T(8,128)S(1)}, u32[]{:S(2)}, u32[]{:S(2)}) collective-permute-start(f32[3,8,18,1]{3,2,1,0:T(8,128)S(1)} %get-tuple-element.15), channel_id=1, source_target_pairs={{0,1},{1,2},{2,3},{3,4},{4,5},{5,6},{6,7},{7,8},{8,9},{9,10},{10,1... | collective-permute-start | bytes 5192 | tf_op jit(solution)/shard_map/ppermute | solution.py:44
  18.9 10.3 %collective-permute-start.3 = (f32[3,8,18,1]{3,2,1,0:T(8,128)S(1)}, f32[3,8,18,1]{3,2,1,0:T(8,128)S(1)}, u32[]{:S(2)}, u32[]{:S(2)}) collective-permute-start(f32[3,8,18,1]{3,2,1,0:T(8,128)S(1)} %get-tuple-element.16), channel_id=1, source_target_pairs={{1,0},{2,1},{3,2},{4,3},{5,4},{6,5},{7,6},{8,7},{9,8},{10,9},{11,1... | collective-permute-start | bytes 5192 | tf_op jit(solution)/shard_map/ppermute | solution.py:45
  30.0 0.8 copy-start.1
  30.8 0.7 copy-start.7
  31.5 0.7 copy-start.5
  32.4 5.9 collective-permute-start.4
  34.3 4.3 collective-permute-start.5
  38.7 9.4 %collective-permute-start.6 = (f32[1,8,18,1]{3,2,1,0:T(8,128)S(1)}, f32[1,8,18,1]{3,2,1,0:T(8,128)S(1)}, u32[]{:S(2)}, u32[]{:S(2)}) collective-permute-start(f32[1,8,18,1]{3,2,1,0:T(8,128)S(1)} %get-tuple-element.32), channel_id=1, source_target_pairs={{0,1},{1,2},{2,3},{3,4},{4,5},{5,6},{6,7},{7,8},{8,9},{9,10},{10,1... | collective-permute-start | bytes 1736 | tf_op jit(solution)/shard_map/ppermute | solution.py:44
  40.6 9.1 %collective-permute-start.7 = (f32[1,8,18,1]{3,2,1,0:T(8,128)S(1)}, f32[1,8,18,1]{3,2,1,0:T(8,128)S(1)}, u32[]{:S(2)}, u32[]{:S(2)}) collective-permute-start(f32[1,8,18,1]{3,2,1,0:T(8,128)S(1)} %get-tuple-element.33), channel_id=1, source_target_pairs={{1,0},{2,1},{3,2},{4,3},{5,4},{6,5},{7,6},{8,7},{9,8},{10,9},{11,1... | collective-permute-start | bytes 1736 | tf_op jit(solution)/shard_map/ppermute | solution.py:45
  50.8 0.8 copy-start.3
  51.6 0.7 copy-start.9
  52.3 0.7 copy-start.8
  53.3 7.1 collective-permute-start.8
  53.3 7.3 collective-permute-start.9
  60.6 9.4 %collective-permute-start.10 = (f32[1,8,18,1]{3,2,1,0:T(8,128)S(1)}, f32[1,8,18,1]{3,2,1,0:T(8,128)S(1)}, u32[]{:S(2)}, u32[]{:S(2)}) collective-permute-start(f32[1,8,18,1]{3,2,1,0:T(8,128)S(1)} %get-tuple-element.30), channel_id=1, source_target_pairs={{0,1},{1,2},{2,3},{3,4},{4,5},{5,6},{6,7},{7,8},{8,9},{9,10},{10,1... | collective-permute-start | bytes 1736 | tf_op jit(solution)/shard_map/ppermute | solution.py:44
  62.6 9.0 %collective-permute-start.11 = (f32[1,8,18,1]{3,2,1,0:T(8,128)S(1)}, f32[1,8,18,1]{3,2,1,0:T(8,128)S(1)}, u32[]{:S(2)}, u32[]{:S(2)}) collective-permute-start(f32[1,8,18,1]{3,2,1,0:T(8,128)S(1)} %get-tuple-element.31), channel_id=1, source_target_pairs={{1,0},{2,1},{3,2},{4,3},{5,4},{6,5},{7,6},{8,7},{9,8},{10,9},{11,1... | collective-permute-start | bytes 1736 | tf_op jit(solution)/shard_map/ppermute | solution.py:45
  284.5 3.1 collective-permute-start.12
  286.8 3.0 collective-permute-start.13
  289.9 10.0 %collective-permute-start.14 = (f32[1,8,18,1]{3,2,1,0:T(8,128)S(1)}, f32[1,8,18,1]{3,2,1,0:T(8,128)S(1)}, u32[]{:S(2)}, u32[]{:S(2)}) collective-permute-start(f32[1,8,18,1]{3,2,1,0:T(8,128)S(1)} %get-tuple-element.28), channel_id=1, source_target_pairs={{0,1},{1,2},{2,3},{3,4},{4,5},{5,6},{6,7},{7,8},{8,9},{9,10},{10,1... | collective-permute-start | bytes 1736 | tf_op jit(solution)/shard_map/ppermute | solution.py:44
  292.2 8.7 collective-permute-start.15
  508.6 2.2 collective-permute-start.16
  510.1 3.1 collective-permute-start.17
  513.3 9.1 %collective-permute-start.18 = (f32[1,8,18,1]{3,2,1,0:T(8,128)S(1)}, f32[1,8,18,1]{3,2,1,0:T(8,128)S(1)}, u32[]{:S(2)}, u32[]{:S(2)}) collective-permute-start(f32[1,8,18,1]{3,2,1,0:T(8,128)S(1)} %get-tuple-element.26), channel_id=1, source_target_pairs={{0,1},{1,2},{2,3},{3,4},{4,5},{5,6},{6,7},{7,8},{8,9},{9,10},{10,1... | collective-permute-start | bytes 1736 | tf_op jit(solution)/shard_map/ppermute | solution.py:44
  515.6 7.9 collective-permute-start.19
  731.9 3.1 collective-permute-start.20
  734.3 3.0 collective-permute-start.21
  737.4 10.0 %collective-permute-start.22 = (f32[1,8,18,1]{3,2,1,0:T(8,128)S(1)}, f32[1,8,18,1]{3,2,1,0:T(8,128)S(1)}, u32[]{:S(2)}, u32[]{:S(2)}) collective-permute-start(f32[1,8,18,1]{3,2,1,0:T(8,128)S(1)} %get-tuple-element.24), channel_id=1, source_target_pairs={{0,1},{1,2},{2,3},{3,4},{4,5},{5,6},{6,7},{7,8},{8,9},{9,10},{10,1... | collective-permute-start | bytes 1736 | tf_op jit(solution)/shard_map/ppermute | solution.py:44
  739.9 8.4 collective-permute-start.23
  853.4 0.6 copy-start.4
  854.3 3.5 collective-permute-start.24
  857.0 3.1 collective-permute-start.25
  860.3 14.0 %collective-permute-start.26 = (f32[3,8,18,1]{3,2,1,0:T(8,128)S(1)}, f32[3,8,18,1]{3,2,1,0:T(8,128)S(1)}, u32[]{:S(2)}, u32[]{:S(2)}) collective-permute-start(f32[3,8,18,1]{3,2,1,0:T(8,128)S(1)} %get-tuple-element.13), channel_id=1, source_target_pairs={{0,1},{1,2},{2,3},{3,4},{4,5},{5,6},{6,7},{7,8},{8,9},{9,10},{10,1... | collective-permute-start | bytes 5192 | tf_op jit(solution)/shard_map/ppermute | solution.py:44
  862.2 13.1 %collective-permute-start.27 = (f32[3,8,18,1]{3,2,1,0:T(8,128)S(1)}, f32[3,8,18,1]{3,2,1,0:T(8,128)S(1)}, u32[]{:S(2)}, u32[]{:S(2)}) collective-permute-start(f32[3,8,18,1]{3,2,1,0:T(8,128)S(1)} %get-tuple-element.14), channel_id=1, source_target_pairs={{1,0},{2,1},{3,2},{4,3},{5,4},{6,5},{7,6},{8,7},{9,8},{10,9},{11,1... | collective-permute-start | bytes 5192 | tf_op jit(solution)/shard_map/ppermute | solution.py:45
where the time goes:
time: 879 us; the launch traced here: 877 us
  blocking collectives  714 us (81%)
  starting transfers between devices  89.1 us (10%)
  waiting for transfers between devices  33.5 us (4%)
  between operations  10.9 us (1%)
  other arithmetic  10 us (1%)
  matrix products  9.55 us (1%)
  local copies, waits for them, and re-layouts  9.23 us (1%)
    psum x3, blocking collectives, solve_pressure(): curve = lax.psum(inner(direction, image, inverse_share), ('gx', 'gy'))  310 us
    psum x3, blocking collectives, solve_pressure(): norm_next = lax.psum(inner(resid, resid, inverse_share), ('gx', 'gy'))  296 us
    psum x1, blocking collectives, solve_pressure(): lax.psum((inner(resid, resid, inverse_share), inner(direction, image, inv...  109 us
    ppermute x14, starting transfers between devices, with_halo(): after = lax.ppermute(initial, axis, down)  60.8 us
    ppermute x14, starting transfers between devices, with_halo(): before = lax.ppermute(last, axis, up)  28.4 us
    ppermute x14, waiting for transfers between devices, with_halo(): after = lax.ppermute(initial, axis, down)  18.2 us
  transfers between devices with their start and end apart: 28, of which 27 were waited for; matrix products, arithmetic and copies ran while one was open for 0% of the time, Pallas kernels for 0%

commit v1 on v0

--- a/solution.py
+++ b/solution.py
@@ -163,7 +163,7 @@
         pressure = pressure + step_length * direction
         resid = resid - step_length * image
         if round_index + 1 < ITERS:
-            norm_next = lax.psum(inner(resid, resid, inverse_share), ("gx", "gy"))
+            norm_next = lax.psum(lax.psum(inner(resid, resid, inverse_share), "gy"), "gx")
             direction = resid + norm_next / norm_now * direction
             norm_now = norm_next
     return pressure

time: 879 us -> 832 us (0.947)
  blocking collectives: 714 us -> 677 us
    psum x3 -> x6, blocking collectives: 296 us -> 252 us  [the longest x3 161 us: solve_pressure(): lax.psum(lax.psum(inner(resid, resid, inverse_share), 'gy'), 'gx')]
where the time goes in v1:
time: 832 us; the launch traced here: 828 us
  blocking collectives  677 us (81%)
  starting transfers between devices  83.6 us (10%)
  waiting for transfers between devices  26.8 us (3%)
  between operations  11 us (1%)
  other arithmetic  10 us (1%)
  matrix products  9.55 us (1%)
  local copies, waits for them, and re-layouts  9.23 us (1%)
    psum x3, blocking collectives, solve_pressure(): curve = lax.psum(inner(direction, image, inverse_share), ('gx', 'gy'))  317 us
    psum x3, blocking collectives, solve_pressure(): lax.psum(lax.psum(inner(resid, resid, inverse_share), 'gy'), 'gx')  161 us
    psum x1, blocking collectives, solve_pressure(): lax.psum((inner(resid, resid, inverse_share), inner(direction, image, inv...  109 us
    psum x3, blocking collectives, solve_pressure(): lax.psum(inner(resid, resid, inverse_share), 'gy')  90.8 us
    ppermute x14, starting transfers between devices, with_halo(): after = lax.ppermute(initial, axis, down)  62.5 us
    ppermute x14, starting transfers between devices, with_halo(): before = lax.ppermute(last, axis, up)  21.1 us
    ppermute x14, waiting for transfers between devices, with_halo(): after = lax.ppermute(initial, axis, down)  17.5 us
  transfers between devices with their start and end apart: 28, of which 27 were waited for; matrix products, arithmetic and copies ran while one was open for 0% of the time, Pallas kernels for 0%

profile of v1, /device:TPU:1, one launch (start us, length us, event | category | flops | bytes accessed | tf_op | source)
XLA Modules:
  0.0 827.5 jit_solution(11909358740170455451)
XLA Ops:
  0.7 0.7 copy-done.11
  1.3 1.3 convolution_bitcast_fusion.3
  6.4 0.7 copy-done.13
  9.0 3.0 collective-permute-start
  12.1 3.9 collective-permute-start.1
  17.0 1.9 collective-permute-start.2
  18.9 6.7 collective-permute-start.3
  25.6 2.2 collective-permute-done.2
  27.8 1.5 collective-permute-done.3
  30.0 0.8 copy-done.1
  32.4 1.8 collective-permute-start.4
  34.3 3.5 collective-permute-start.5
  37.8 0.6 collective-permute-done.4
  38.7 1.9 collective-permute-start.6
  40.6 7.4 collective-permute-start.7
  48.1 1.6 collective-permute-done.7
  50.9 0.7 copy-done.3
  53.3 6.4 collective-permute-start.9
  59.7 0.6 collective-permute-done.8
  60.6 1.9 collective-permute-start.10
  62.6 7.4 collective-permute-start.11
  70.0 1.6 collective-permute-done.11
  71.8 0.8 multiply_reduce_fusion.5
  72.6 108.5 %all-reduce = (f32[]{:T(128)}, f32[]{:T(128)}) all-reduce(f32[]{:T(128)} %get-tuple-element.3, f32[]{:T(128)} %get-tuple-element.2), channel_id=1, replica_groups=mesh['gx'=32,'gy'=16] {'gx','gy'}, use_global_device_ids=true, to_apply=%region_4.5 | all-reduce | flops 2 | bytes 16 | tf_op jit(solution)/shard_map/psum | solution.py:156
  182.5 0.7 multiply_reduce_fusion.4
  183.2 30.3 %psum.79 = f32[]{:T(128)} all-reduce(f32[]{:T(128)} %multiply_reduce_fusion.4), channel_id=1, replica_groups=mesh['gx'=32,'gy'=16] {'gy'}, use_global_device_ids=true, to_apply=%region_8.9 | all-reduce | flops 1 | bytes 8 | tf_op jit(solution)/shard_map/psum | solution.py:166
  213.5 53.7 %psum.80 = f32[]{:T(128)} all-reduce(f32[]{:T(128)} %psum.79), channel_id=1, replica_groups=mesh['gx'=32,'gy'=16] {'gx'}, use_global_device_ids=true, to_apply=%region_9.10 | all-reduce | flops 1 | bytes 8 | tf_op jit(solution)/shard_map/psum | solution.py:166
  270.0 0.7 collective-permute-start.13
  270.7 0.6 collective-permute-done.12
  271.3 1.8 collective-permute-done.13
  273.2 2.5 collective-permute-start.14
  275.7 6.1 collective-permute-start.15
  281.8 1.6 collective-permute-done.15
  283.7 0.7 multiply_reduce_fusion.3
  284.4 105.6 %psum.81 = f32[]{:T(128)} all-reduce(f32[]{:T(128)} %get-tuple-element.10), channel_id=1, replica_groups=mesh['gx'=32,'gy'=16] {'gx','gy'}, use_global_device_ids=true, to_apply=%region_11.12 | all-reduce | flops 1 | bytes 8 | tf_op jit(solution)/shard_map/psum | solution.py:161
  391.3 0.7 multiply_reduce_fusion.2
  392.0 30.3 %psum.82 = f32[]{:T(128)} all-reduce(f32[]{:T(128)} %get-tuple-element.8), channel_id=1, replica_groups=mesh['gx'=32,'gy'=16] {'gy'}, use_global_device_ids=true, to_apply=%region_13.14 | all-reduce | flops 1 | bytes 8 | tf_op jit(solution)/shard_map/psum | solution.py:166
  422.3 53.7 %psum.83 = f32[]{:T(128)} all-reduce(f32[]{:T(128)} %psum.82), channel_id=1, replica_groups=mesh['gx'=32,'gy'=16] {'gx'}, use_global_device_ids=true, to_apply=%region_14.15 | all-reduce | flops 1 | bytes 8 | tf_op jit(solution)/shard_map/psum | solution.py:166
  478.7 0.7 collective-permute-start.17
  479.4 0.6 collective-permute-done.16
  480.0 1.7 collective-permute-done.17
  481.9 2.7 collective-permute-start.18
  484.6 5.9 collective-permute-start.19
  490.6 1.6 collective-permute-done.19
  492.4 0.7 multiply_reduce_fusion.1
  493.1 105.6 %psum.84 = f32[]{:T(128)} all-reduce(f32[]{:T(128)} %get-tuple-element.6), channel_id=1, replica_groups=mesh['gx'=32,'gy'=16] {'gx','gy'}, use_global_device_ids=true, to_apply=%region_16.17 | all-reduce | flops 1 | bytes 8 | tf_op jit(solution)/shard_map/psum | solution.py:161
  600.7 30.3 %psum.85 = f32[]{:T(128)} all-reduce(f32[]{:T(128)} %multiply_reduce_fusion), channel_id=1, replica_groups=mesh['gx'=32,'gy'=16] {'gy'}, use_global_device_ids=true, to_apply=%region_18.19 | all-reduce | flops 1 | bytes 8 | tf_op jit(solution)/shard_map/psum | solution.py:166
  630.9 53.9 %psum.86 = f32[]{:T(128)} all-reduce(f32[]{:T(128)} %psum.85), channel_id=1, replica_groups=mesh['gx'=32,'gy'=16] {'gx'}, use_global_device_ids=true, to_apply=%region_19.20 | all-reduce | flops 1 | bytes 8 | tf_op jit(solution)/shard_map/psum | solution.py:166
  687.6 0.7 collective-permute-start.21
  688.2 0.6 collective-permute-done.20
  688.9 1.7 collective-permute-done.21
  690.7 2.7 collective-permute-start.22
  693.4 5.9 collective-permute-start.23
  699.4 1.6 collective-permute-done.23
  701.2 0.7 fusion.73
  701.9 105.6 %psum.87 = f32[]{:T(128)} all-reduce(f32[]{:T(128)} %fusion.73), channel_id=1, replica_groups=mesh['gx'=32,'gy'=16] {'gx','gy'}, use_global_device_ids=true, to_apply=%region_21.22 | all-reduce | flops 1 | bytes 8 | tf_op jit(solution)/shard_map/psum | solution.py:161
  810.2 0.9 collective-permute-start.25
  811.1 0.6 collective-permute-done.24
  811.8 1.5 collective-permute-done.25
  813.5 2.1 collective-permute-start.26
  815.7 6.5 collective-permute-start.27
  822.1 3.0 collective-permute-done.26
  825.1 0.9 collective-permute-done.27
  826.6 1.0 fusion.35
  (162 shorter events, 20.6 us)
Async XLA Ops:
  0.6 0.7 copy-start.11
  1.3 1.3 copy-start
  1.3 1.3 copy-start.2
  2.7 0.8 copy-start.6
  4.1 0.7 copy-start.15
  4.9 0.7 copy-start.12
  6.4 0.7 copy-start.13
  7.1 0.7 copy-start.14
  7.7 0.8 copy-start.10
  9.0 7.6 collective-permute-start
  12.1 3.9 copy-start.16
  12.1 4.7 collective-permute-start.1
  17.0 10.8 %collective-permute-start.2 = (f32[3,8,18,1]{3,2,1,0:T(8,128)S(1)}, f32[3,8,18,1]{3,2,1,0:T(8,128)S(1)}, u32[]{:S(2)}, u32[]{:S(2)}) collective-permute-start(f32[3,8,18,1]{3,2,1,0:T(8,128)S(1)} %get-tuple-element.15), channel_id=1, source_target_pairs={{0,1},{1,2},{2,3},{3,4},{4,5},{5,6},{6,7},{7,8},{8,9},{9,10},{10,1... | collective-permute-start | bytes 5192 | tf_op jit(solution)/shard_map/ppermute | solution.py:44
  18.9 10.3 %collective-permute-start.3 = (f32[3,8,18,1]{3,2,1,0:T(8,128)S(1)}, f32[3,8,18,1]{3,2,1,0:T(8,128)S(1)}, u32[]{:S(2)}, u32[]{:S(2)}) collective-permute-start(f32[3,8,18,1]{3,2,1,0:T(8,128)S(1)} %get-tuple-element.16), channel_id=1, source_target_pairs={{1,0},{2,1},{3,2},{4,3},{5,4},{6,5},{7,6},{8,7},{9,8},{10,9},{11,1... | collective-permute-start | bytes 5192 | tf_op jit(solution)/shard_map/ppermute | solution.py:45
  30.0 0.8 copy-start.1
  30.8 0.7 copy-start.7
  31.5 0.7 copy-start.5
  32.4 5.9 collective-permute-start.4
  34.3 4.3 collective-permute-start.5
  38.7 9.4 %collective-permute-start.6 = (f32[1,8,18,1]{3,2,1,0:T(8,128)S(1)}, f32[1,8,18,1]{3,2,1,0:T(8,128)S(1)}, u32[]{:S(2)}, u32[]{:S(2)}) collective-permute-start(f32[1,8,18,1]{3,2,1,0:T(8,128)S(1)} %get-tuple-element.32), channel_id=1, source_target_pairs={{0,1},{1,2},{2,3},{3,4},{4,5},{5,6},{6,7},{7,8},{8,9},{9,10},{10,1... | collective-permute-start | bytes 1736 | tf_op jit(solution)/shard_map/ppermute | solution.py:44
  40.6 9.1 %collective-permute-start.7 = (f32[1,8,18,1]{3,2,1,0:T(8,128)S(1)}, f32[1,8,18,1]{3,2,1,0:T(8,128)S(1)}, u32[]{:S(2)}, u32[]{:S(2)}) collective-permute-start(f32[1,8,18,1]{3,2,1,0:T(8,128)S(1)} %get-tuple-element.33), channel_id=1, source_target_pairs={{1,0},{2,1},{3,2},{4,3},{5,4},{6,5},{7,6},{8,7},{9,8},{10,9},{11,1... | collective-permute-start | bytes 1736 | tf_op jit(solution)/shard_map/ppermute | solution.py:45
  50.8 0.8 copy-start.3
  51.6 0.7 copy-start.9
  52.3 0.7 copy-start.8
  53.3 7.1 collective-permute-start.8
  53.3 7.3 collective-permute-start.9
  60.6 9.4 %collective-permute-start.10 = (f32[1,8,18,1]{3,2,1,0:T(8,128)S(1)}, f32[1,8,18,1]{3,2,1,0:T(8,128)S(1)}, u32[]{:S(2)}, u32[]{:S(2)}) collective-permute-start(f32[1,8,18,1]{3,2,1,0:T(8,128)S(1)} %get-tuple-element.30), channel_id=1, source_target_pairs={{0,1},{1,2},{2,3},{3,4},{4,5},{5,6},{6,7},{7,8},{8,9},{9,10},{10,1... | collective-permute-start | bytes 1736 | tf_op jit(solution)/shard_map/ppermute | solution.py:44
  62.6 9.0 %collective-permute-start.11 = (f32[1,8,18,1]{3,2,1,0:T(8,128)S(1)}, f32[1,8,18,1]{3,2,1,0:T(8,128)S(1)}, u32[]{:S(2)}, u32[]{:S(2)}) collective-permute-start(f32[1,8,18,1]{3,2,1,0:T(8,128)S(1)} %get-tuple-element.31), channel_id=1, source_target_pairs={{1,0},{2,1},{3,2},{4,3},{5,4},{6,5},{7,6},{8,7},{9,8},{10,9},{11,1... | collective-permute-start | bytes 1736 | tf_op jit(solution)/shard_map/ppermute | solution.py:45
  270.0 1.3 collective-permute-start.12
  270.0 3.0 collective-permute-start.13
  273.2 8.7 %collective-permute-start.14 = (f32[1,8,18,1]{3,2,1,0:T(8,128)S(1)}, f32[1,8,18,1]{3,2,1,0:T(8,128)S(1)}, u32[]{:S(2)}, u32[]{:S(2)}) collective-permute-start(f32[1,8,18,1]{3,2,1,0:T(8,128)S(1)} %get-tuple-element.28), channel_id=1, source_target_pairs={{0,1},{1,2},{2,3},{3,4},{4,5},{5,6},{6,7},{7,8},{8,9},{9,10},{10,1... | collective-permute-start | bytes 1736 | tf_op jit(solution)/shard_map/ppermute | solution.py:44
  275.7 7.7 collective-permute-start.15
  478.7 1.3 collective-permute-start.16
  478.7 3.0 collective-permute-start.17
  481.9 8.7 %collective-permute-start.18 = (f32[1,8,18,1]{3,2,1,0:T(8,128)S(1)}, f32[1,8,18,1]{3,2,1,0:T(8,128)S(1)}, u32[]{:S(2)}, u32[]{:S(2)}) collective-permute-start(f32[1,8,18,1]{3,2,1,0:T(8,128)S(1)} %get-tuple-element.26), channel_id=1, source_target_pairs={{0,1},{1,2},{2,3},{3,4},{4,5},{5,6},{6,7},{7,8},{8,9},{9,10},{10,1... | collective-permute-start | bytes 1736 | tf_op jit(solution)/shard_map/ppermute | solution.py:44
  484.6 7.5 collective-permute-start.19
  687.5 1.3 collective-permute-start.20
  687.6 3.0 collective-permute-start.21
  690.7 8.7 %collective-permute-start.22 = (f32[1,8,18,1]{3,2,1,0:T(8,128)S(1)}, f32[1,8,18,1]{3,2,1,0:T(8,128)S(1)}, u32[]{:S(2)}, u32[]{:S(2)}) collective-permute-start(f32[1,8,18,1]{3,2,1,0:T(8,128)S(1)} %get-tuple-element.24), channel_id=1, source_target_pairs={{0,1},{1,2},{2,3},{3,4},{4,5},{5,6},{6,7},{7,8},{8,9},{9,10},{10,1... | collective-permute-start | bytes 1736 | tf_op jit(solution)/shard_map/ppermute | solution.py:44
  693.4 7.5 collective-permute-start.23
  809.0 0.6 copy-start.4
  809.9 1.9 collective-permute-start.24
  810.2 3.1 collective-permute-start.25
  813.5 11.6 %collective-permute-start.26 = (f32[3,8,18,1]{3,2,1,0:T(8,128)S(1)}, f32[3,8,18,1]{3,2,1,0:T(8,128)S(1)}, u32[]{:S(2)}, u32[]{:S(2)}) collective-permute-start(f32[3,8,18,1]{3,2,1,0:T(8,128)S(1)} %get-tuple-element.13), channel_id=1, source_target_pairs={{0,1},{1,2},{2,3},{3,4},{4,5},{5,6},{6,7},{7,8},{8,9},{9,10},{10,1... | collective-permute-start | bytes 5192 | tf_op jit(solution)/shard_map/ppermute | solution.py:44
  815.7 10.4 %collective-permute-start.27 = (f32[3,8,18,1]{3,2,1,0:T(8,128)S(1)}, f32[3,8,18,1]{3,2,1,0:T(8,128)S(1)}, u32[]{:S(2)}, u32[]{:S(2)}) collective-permute-start(f32[3,8,18,1]{3,2,1,0:T(8,128)S(1)} %get-tuple-element.14), channel_id=1, source_target_pairs={{1,0},{2,1},{3,2},{4,3},{5,4},{6,5},{7,6},{8,7},{9,8},{10,9},{11,1... | collective-permute-start | bytes 5192 | tf_op jit(solution)/shard_map/ppermute | solution.py:45
